TPU v7x, 256 devices: a whole 4x4x8 slice. The times are simulated.
256 devices in a mesh: section: 16 (over z, core), dp: 16 (over y, x).
Axes of the slice: x: 4, y: 4, z: 8, core: 2. Of those that a mesh axis runs over, the one named last changes fastest.
Arguments:
- layer_inputs: bfloat16 [16, 16, 1024, 4096], P('section', 'dp'), may hold values from -2.5 to 2.5
- keys_values: bfloat16 [16, 16, 1024, 1024], P('section', 'dp'), may hold values from -2.5 to 2.5
- loss_weight: float32 [16, 1024], P('dp'), may hold values from 0.25 to 4
- doc_ids: int32 [16, 8, 128], replicated, may hold values from 0 to 3, never falling along the last dimension, each value on 1 to 64 neighbouring positions
- assignment: int32 [16, 8], replicated, may hold values from 0 to 15, as said below
Outputs:
- key_value_grads: bfloat16 [16, 16, 1024, 1024], P('section', 'dp')
Inputs may be any that keep to these rules, and one draw needn't show every extreme that they name: For every microbatch m the column assignment[:, m] is a permutation of the replicas, and no replica hands more than 1 of its microbatches to one replica. `doc_ids`: within a microbatch the ids never fall; a document has at most 64 positions.
All inputs are finite; a program needn't handle non-finite values.
Results may differ from a plain program's by a relative error of at most 0.0097.
Values may be sent and summed in bfloat16 or wider, within the bound.
A program may use at most 128 MiB of HBM per device.

v0:
```python
import jax
import jax.numpy as jnp
from jax import lax
from jax.sharding import PartitionSpec as P

KV_HEADS = 4
HEAD_DIM = 128


def from_behind(block, axis, distance):
    devices = range(lax.axis_size(axis))
    route = [(i - distance, i) for i in devices if i - distance in devices]
    return lax.ppermute(block, axis, route)


def source_of(assignment, worker):
    replica_ids = jnp.arange(assignment.shape[0], dtype=jnp.int32)
    return jnp.sum(jnp.where(assignment == worker, replica_ids[:, None], 0), axis=0)


def earlier_count(labels):
    position_ids = jnp.arange(labels.shape[0], dtype=jnp.int32)
    before = (labels[None, :] == labels[:, None]) & (position_ids[None, :] < position_ids[:, None])
    return jnp.sum(before, axis=1)


def mask_of(documents):
    positions = jnp.arange(documents.shape[0], dtype=jnp.int32)
    return (documents[:, None] == documents[None, :]) & (positions[None, :] <= positions[:, None])


def pick_row(source_array, slot_index):
    return lax.dynamic_index_in_dim(source_array, slot_index, 0, keepdims=False)


def heads_of(queries, gathered):
    query_heads = queries.reshape(queries.shape[0], KV_HEADS, -1, HEAD_DIM)
    key_heads = gathered[:, : KV_HEADS * HEAD_DIM].reshape(-1, KV_HEADS, HEAD_DIM)
    value_heads = gathered[:, KV_HEADS * HEAD_DIM :].reshape(-1, KV_HEADS, HEAD_DIM)
    return (query_heads, key_heads, value_heads)


def attention_weights(query_heads, key_heads, allowed):
    scores = jnp.einsum(
        "ikgd,jkd->kgij", query_heads, key_heads, preferred_element_type=jnp.float32
    ) * HEAD_DIM ** (-0.5)
    soft = jnp.where(allowed[None, None], jnp.exp(scores), 0.0)
    return soft / jnp.sum(soft, axis=-1, keepdims=True)


def top_grad(queries, gathered, allowed, weights):
    query_heads, key_heads, value_heads = heads_of(queries, gathered)
    soft_weights = attention_weights(query_heads, key_heads, allowed)
    mixed_out = jnp.einsum(
        "kgij,jkd->ikgd",
        soft_weights.astype(jnp.bfloat16),
        value_heads,
        preferred_element_type=jnp.float32,
    )
    output_sum = queries.astype(jnp.float32) + mixed_out.reshape(queries.shape[0], -1)
    return (weights[:, None] * output_sum).astype(jnp.bfloat16)


def tile_backward(queries, gathered, allowed, upstream):
    query_heads, key_heads, value_heads = heads_of(queries, gathered)
    soft_weights = attention_weights(query_heads, key_heads, allowed)
    grad_heads = upstream.reshape(upstream.shape[0], KV_HEADS, -1, HEAD_DIM)
    dprobs = jnp.einsum(
        "ikgd,jkd->kgij", grad_heads, value_heads, preferred_element_type=jnp.float32
    )
    row_delta = jnp.sum(soft_weights * dprobs, axis=-1, keepdims=True)
    dscores = (soft_weights * (dprobs - row_delta)).astype(jnp.bfloat16)
    score_scale = HEAD_DIM ** (-0.5)
    dquery = (
        jnp.einsum("kgij,jkd->ikgd", dscores, key_heads, preferred_element_type=jnp.float32)
        * score_scale
    )
    key_grad = (
        jnp.einsum("kgij,ikgd->jkd", dscores, query_heads, preferred_element_type=jnp.float32)
        * score_scale
    )
    value_grad = jnp.einsum(
        "kgij,ikgd->jkd",
        soft_weights.astype(jnp.bfloat16),
        grad_heads,
        preferred_element_type=jnp.float32,
    )
    key_rows = gathered.shape[0]
    key_terms = jnp.concatenate(
        [key_grad.reshape(key_rows, -1), value_grad.reshape(key_rows, -1)], axis=-1
    )
    return (dquery.reshape(queries.shape[0], -1), key_terms)


def on_device(layer_inputs, keys_values, loss_weight, doc_ids, assignment):
    sections = lax.axis_size("section")
    replicas = lax.axis_size("dp")
    section_index = lax.axis_index("section")
    my_index = lax.axis_index("dp")
    micro_count = assignment.shape[1]
    capacity = (micro_count + replicas - 1) // replicas
    rows_tile = layer_inputs.shape[2] // micro_count
    features = layer_inputs.shape[-1]
    kv_features = keys_values.shape[-1]
    micro_index = jnp.arange(micro_count, dtype=jnp.int32)
    targets = lax.dynamic_index_in_dim(assignment, my_index, 0, keepdims=False)
    placing = targets * capacity + earlier_count(targets)
    send_index = (
        jnp.full((replicas * capacity,), micro_count, jnp.int32).at[placing].set(micro_index)
    )
    own_kv = keys_values[0, 0].reshape(micro_count, rows_tile, kv_features)
    padded = jnp.concatenate([own_kv, jnp.zeros_like(own_kv[:1])], axis=0)
    outgoing = jnp.take(padded, send_index, axis=0).reshape(
        replicas, capacity, rows_tile, kv_features
    )
    arrived = lax.all_to_all(outgoing, "dp", split_axis=0, concat_axis=0, tiled=True)
    sources = source_of(assignment, my_index)
    picked = sources * capacity + earlier_count(sources)
    run_kv = jnp.take(arrived.reshape(replicas * capacity, rows_tile, kv_features), picked, axis=0)
    run_docs = doc_ids[sources, micro_index]
    allowed = jax.vmap(mask_of)(run_docs)
    queries = layer_inputs[0, 0].reshape(micro_count, rows_tile, features)
    weights = loss_weight[0].reshape(micro_count, rows_tile)
    is_top = section_index == sections - 1
    top_seed = lax.cond(
        is_top,
        lambda: lax.map(lambda packed: top_grad(*packed), (queries, run_kv, allowed, weights)),
        lambda: jnp.zeros(queries.shape, jnp.bfloat16),
    )
    pieces = 1
    block_rows = rows_tile // pieces
    unit_count = micro_count * pieces
    tick_count = sections + unit_count - 1

    def advance(counter, state_pair):
        passing, results = state_pair
        received = from_behind(passing, "section", -1)
        current = counter - (sections - 1 - section_index)
        active = (current >= 0) & (current < unit_count)
        clamped = jnp.clip(current, 0, unit_count - 1)
        micro_slot = clamped // pieces
        offset = clamped % pieces * block_rows

        def backward_unit(operands):
            passing_old, results_old = operands
            tile_queries = pick_row(queries, micro_slot)
            tile_allowed = pick_row(allowed, micro_slot)
            seeded = pick_row(top_seed, micro_slot)
            upstream = jnp.where(is_top, seeded, received)
            dquery, key_terms = tile_backward(
                tile_queries, pick_row(run_kv, micro_slot), tile_allowed, upstream
            )
            passed = (upstream.astype(jnp.float32) + dquery).astype(jnp.bfloat16)
            updated = lax.dynamic_update_index_in_dim(
                results_old, pick_row(results_old, micro_slot) + key_terms, micro_slot, 0
            )
            return (passed, updated)

        return lax.cond(active, backward_unit, lambda operands: operands, (passing, results))

    initial = (
        jnp.zeros((block_rows, features), jnp.bfloat16),
        jnp.zeros((micro_count, rows_tile, kv_features), jnp.float32),
    )
    _, results = lax.fori_loop(0, tick_count, advance, initial)
    return results.astype(jnp.bfloat16).reshape(1, 1, micro_count * rows_tile, kv_features)


def solution(mesh):
    placed = (
        P("section", "dp", None, None),
        P("section", "dp", None, None),
        P("dp", None),
        P(),
        P(),
    )
    return jax.shard_map(
        on_device,
        mesh=mesh,
        in_specs=placed,
        out_specs=P("section", "dp", None, None),
        check_vma=False,
    )
```

profile of v0, /device:TPU:1, one launch (start us, length us, event | category | flops | bytes accessed | tf_op | source)
XLA Modules:
  0.0 639.1 jit_solution(15784955764810483193)
XLA Ops:
  3.6 2.8 gather_fusion
  6.4 4.6 bitcast_select_fusion.3
  11.0 7.6 %all-to-all-start = ((bf16[16,1,128,1024]{3,2,1,0:T(8,128)(2,1)}), bf16[16,1,128,1024]{3,2,1,0:T(8,128)(2,1)}, u32[]{:S(2)}, u32[]{:S(2)}) async-start(bf16[16,1,128,1024]{3,2,1,0:T(8,128)(2,1)} %bitcast_select_fusion.3), calls=%async_computation | async-start | bytes 8388608 | tf_op jit(solution)/shard_map/all_to_all | solution.py:116
  18.7 11.9 %copy.71 = bf16[8,128,4096]{1,2,0:T(8,128)(2,1)} copy(bf16[8,128,4096]{2,1,0:T(8,128)(2,1)} %bitcast.163) | data formatting | bytes 16777216
  31.8 49.2 %all-to-all-done = bf16[16,1,128,1024]{3,2,1,0:T(8,128)(2,1)} async-done(((bf16[16,1,128,1024]{3,2,1,0:T(8,128)(2,1)}), bf16[16,1,128,1024]{3,2,1,0:T(8,128)(2,1)}, u32[]{:S(2)}, u32[]{:S(2)}) %all-to-all-start) | async-done | bytes 4194336 | tf_op jit(solution)/shard_map/all_to_all | solution.py:116
  81.0 2.9 gather_fusion.1
  85.5 3.9 copy.70
  89.4 4.3 conditional.2
  89.4 4.3 broadcast.138
  93.7 2.3 broadcast_in_dim.99
  96.1 537.8 %while.28 = (s32[]{:T(128)}, bf16[128,4096]{0,1:T(8,128)(2,1)S(1)}, f32[8,128,1024]{1,2,0:T(8,128)}, s32[]{:T(128)}, pred[]{:T(512)}, /*index=5*/bf16[8,128,4096...) while((s32[]{:T(128)}, bf16[128,4096]{0,1:T(8,128)(2,1)S(1)}, ...), condition=%wide.region_14.15_spmd.clone, body=%wide.region_9.14_spmd.clone.sunk | while | flops 683499520 | bytes 39390576 | solution.py:165
  96.1 3.7 collective-permute-start
  99.9 14.0 %collective-permute-done = bf16[128,4096]{0,1:T(8,128)(2,1)S(1)} collective-permute-done((bf16[128,4096]{0,1:T(8,128)(2,1)S(1)}, bf16[128,4096]{0,1:T(8,128)(2,1)S(1)}, u32[]{:S(2)}, u32[]{:S(2)}) %collective-permute-start) | collective-permute-done | bytes 1048608 | tf_op jit(solution)/shard_map/while/body/eval_jaxpr/ppermute | solution.py:13
  115.8 14.2 %collective-permute-done = bf16[128,4096]{0,1:T(8,128)(2,1)S(1)} collective-permute-done((bf16[128,4096]{0,1:T(8,128)(2,1)S(1)}, bf16[128,4096]{0,1:T(8,128)(2,1)S(1)}, u32[]{:S(2)}, u32[]{:S(2)}) %collective-permute-start) | collective-permute-done | bytes 1048608 | tf_op jit(solution)/shard_map/while/body/eval_jaxpr/ppermute | solution.py:13
  131.9 14.2 %collective-permute-done = bf16[128,4096]{0,1:T(8,128)(2,1)S(1)} collective-permute-done((bf16[128,4096]{0,1:T(8,128)(2,1)S(1)}, bf16[128,4096]{0,1:T(8,128)(2,1)S(1)}, u32[]{:S(2)}, u32[]{:S(2)}) %collective-permute-start) | collective-permute-done | bytes 1048608 | tf_op jit(solution)/shard_map/while/body/eval_jaxpr/ppermute | solution.py:13
  148.0 14.2 %collective-permute-done = bf16[128,4096]{0,1:T(8,128)(2,1)S(1)} collective-permute-done((bf16[128,4096]{0,1:T(8,128)(2,1)S(1)}, bf16[128,4096]{0,1:T(8,128)(2,1)S(1)}, u32[]{:S(2)}, u32[]{:S(2)}) %collective-permute-start) | collective-permute-done | bytes 1048608 | tf_op jit(solution)/shard_map/while/body/eval_jaxpr/ppermute | solution.py:13
  164.1 14.2 %collective-permute-done = bf16[128,4096]{0,1:T(8,128)(2,1)S(1)} collective-permute-done((bf16[128,4096]{0,1:T(8,128)(2,1)S(1)}, bf16[128,4096]{0,1:T(8,128)(2,1)S(1)}, u32[]{:S(2)}, u32[]{:S(2)}) %collective-permute-start) | collective-permute-done | bytes 1048608 | tf_op jit(solution)/shard_map/while/body/eval_jaxpr/ppermute | solution.py:13
  180.2 14.2 %collective-permute-done = bf16[128,4096]{0,1:T(8,128)(2,1)S(1)} collective-permute-done((bf16[128,4096]{0,1:T(8,128)(2,1)S(1)}, bf16[128,4096]{0,1:T(8,128)(2,1)S(1)}, u32[]{:S(2)}, u32[]{:S(2)}) %collective-permute-start) | collective-permute-done | bytes 1048608 | tf_op jit(solution)/shard_map/while/body/eval_jaxpr/ppermute | solution.py:13
  196.3 14.2 %collective-permute-done = bf16[128,4096]{0,1:T(8,128)(2,1)S(1)} collective-permute-done((bf16[128,4096]{0,1:T(8,128)(2,1)S(1)}, bf16[128,4096]{0,1:T(8,128)(2,1)S(1)}, u32[]{:S(2)}, u32[]{:S(2)}) %collective-permute-start) | collective-permute-done | bytes 1048608 | tf_op jit(solution)/shard_map/while/body/eval_jaxpr/ppermute | solution.py:13
  212.4 14.2 %collective-permute-done = bf16[128,4096]{0,1:T(8,128)(2,1)S(1)} collective-permute-done((bf16[128,4096]{0,1:T(8,128)(2,1)S(1)}, bf16[128,4096]{0,1:T(8,128)(2,1)S(1)}, u32[]{:S(2)}, u32[]{:S(2)}) %collective-permute-start) | collective-permute-done | bytes 1048608 | tf_op jit(solution)/shard_map/while/body/eval_jaxpr/ppermute | solution.py:13
  228.5 14.2 %collective-permute-done = bf16[128,4096]{0,1:T(8,128)(2,1)S(1)} collective-permute-done((bf16[128,4096]{0,1:T(8,128)(2,1)S(1)}, bf16[128,4096]{0,1:T(8,128)(2,1)S(1)}, u32[]{:S(2)}, u32[]{:S(2)}) %collective-permute-start) | collective-permute-done | bytes 1048608 | tf_op jit(solution)/shard_map/while/body/eval_jaxpr/ppermute | solution.py:13
  244.6 14.2 %collective-permute-done = bf16[128,4096]{0,1:T(8,128)(2,1)S(1)} collective-permute-done((bf16[128,4096]{0,1:T(8,128)(2,1)S(1)}, bf16[128,4096]{0,1:T(8,128)(2,1)S(1)}, u32[]{:S(2)}, u32[]{:S(2)}) %collective-permute-start) | collective-permute-done | bytes 1048608 | tf_op jit(solution)/shard_map/while/body/eval_jaxpr/ppermute | solution.py:13
  260.7 14.2 %collective-permute-done = bf16[128,4096]{0,1:T(8,128)(2,1)S(1)} collective-permute-done((bf16[128,4096]{0,1:T(8,128)(2,1)S(1)}, bf16[128,4096]{0,1:T(8,128)(2,1)S(1)}, u32[]{:S(2)}, u32[]{:S(2)}) %collective-permute-start) | collective-permute-done | bytes 1048608 | tf_op jit(solution)/shard_map/while/body/eval_jaxpr/ppermute | solution.py:13
  276.9 14.2 %collective-permute-done = bf16[128,4096]{0,1:T(8,128)(2,1)S(1)} collective-permute-done((bf16[128,4096]{0,1:T(8,128)(2,1)S(1)}, bf16[128,4096]{0,1:T(8,128)(2,1)S(1)}, u32[]{:S(2)}, u32[]{:S(2)}) %collective-permute-start) | collective-permute-done | bytes 1048608 | tf_op jit(solution)/shard_map/while/body/eval_jaxpr/ppermute | solution.py:13
  293.0 14.2 %collective-permute-done = bf16[128,4096]{0,1:T(8,128)(2,1)S(1)} collective-permute-done((bf16[128,4096]{0,1:T(8,128)(2,1)S(1)}, bf16[128,4096]{0,1:T(8,128)(2,1)S(1)}, u32[]{:S(2)}, u32[]{:S(2)}) %collective-permute-start) | collective-permute-done | bytes 1048608 | tf_op jit(solution)/shard_map/while/body/eval_jaxpr/ppermute | solution.py:13
  309.1 14.2 %collective-permute-done = bf16[128,4096]{0,1:T(8,128)(2,1)S(1)} collective-permute-done((bf16[128,4096]{0,1:T(8,128)(2,1)S(1)}, bf16[128,4096]{0,1:T(8,128)(2,1)S(1)}, u32[]{:S(2)}, u32[]{:S(2)}) %collective-permute-start) | collective-permute-done | bytes 1048608 | tf_op jit(solution)/shard_map/while/body/eval_jaxpr/ppermute | solution.py:13
  325.2 95.8 %collective-permute-done = bf16[128,4096]{0,1:T(8,128)(2,1)S(1)} collective-permute-done((bf16[128,4096]{0,1:T(8,128)(2,1)S(1)}, bf16[128,4096]{0,1:T(8,128)(2,1)S(1)}, u32[]{:S(2)}, u32[]{:S(2)}) %collective-permute-start) | collective-permute-done | bytes 1048608 | tf_op jit(solution)/shard_map/while/body/eval_jaxpr/ppermute | solution.py:13
  421.0 9.4 %conditional.5 = ((bf16[128,4096]{0,1:T(8,128)(2,1)S(1)}, f32[8,128,1024]{1,2,0:T(8,128)})) conditional(s32[]{:T(128)} %convert_element_type.77, (bf16[128,4096]{0,1:T(8,128)(2,1)S(1)}, f32[8,128,1024]{1,2,0:T(8,128)}) %tuple.99, (pred[]{:T(512)}, s32[]{:T(128)}, bf16[8,128,4096]{1,2,0:T(8,128)(2,1)}, bf16[128,4096]{0,1:T(8,128)(2,1)S(1)}, ...), branch_computations={%region_10.10_spmd, %region_11.13_spmd} | conditional | flops 683499520 | bytes 35195972 | solution.py:159
  432.3 15.4 %collective-permute-done = bf16[128,4096]{0,1:T(8,128)(2,1)S(1)} collective-permute-done((bf16[128,4096]{0,1:T(8,128)(2,1)S(1)}, bf16[128,4096]{0,1:T(8,128)(2,1)S(1)}, u32[]{:S(2)}, u32[]{:S(2)}) %collective-permute-start) | collective-permute-done | bytes 1048608 | tf_op jit(solution)/shard_map/while/body/eval_jaxpr/ppermute | solution.py:13
  447.7 9.4 %conditional.5 = ((bf16[128,4096]{0,1:T(8,128)(2,1)S(1)}, f32[8,128,1024]{1,2,0:T(8,128)})) conditional(s32[]{:T(128)} %convert_element_type.77, (bf16[128,4096]{0,1:T(8,128)(2,1)S(1)}, f32[8,128,1024]{1,2,0:T(8,128)}) %tuple.99, (pred[]{:T(512)}, s32[]{:T(128)}, bf16[8,128,4096]{1,2,0:T(8,128)(2,1)}, bf16[128,4096]{0,1:T(8,128)(2,1)S(1)}, ...), branch_computations={%region_10.10_spmd, %region_11.13_spmd} | conditional | flops 683499520 | bytes 35195972 | solution.py:159
  459.1 15.5 %collective-permute-done = bf16[128,4096]{0,1:T(8,128)(2,1)S(1)} collective-permute-done((bf16[128,4096]{0,1:T(8,128)(2,1)S(1)}, bf16[128,4096]{0,1:T(8,128)(2,1)S(1)}, u32[]{:S(2)}, u32[]{:S(2)}) %collective-permute-start) | collective-permute-done | bytes 1048608 | tf_op jit(solution)/shard_map/while/body/eval_jaxpr/ppermute | solution.py:13
  474.6 9.4 %conditional.5 = ((bf16[128,4096]{0,1:T(8,128)(2,1)S(1)}, f32[8,128,1024]{1,2,0:T(8,128)})) conditional(s32[]{:T(128)} %convert_element_type.77, (bf16[128,4096]{0,1:T(8,128)(2,1)S(1)}, f32[8,128,1024]{1,2,0:T(8,128)}) %tuple.99, (pred[]{:T(512)}, s32[]{:T(128)}, bf16[8,128,4096]{1,2,0:T(8,128)(2,1)}, bf16[128,4096]{0,1:T(8,128)(2,1)S(1)}, ...), branch_computations={%region_10.10_spmd, %region_11.13_spmd} | conditional | flops 683499520 | bytes 35195972 | solution.py:159
  481.5 1.9 fusion.18
  486.0 15.4 %collective-permute-done = bf16[128,4096]{0,1:T(8,128)(2,1)S(1)} collective-permute-done((bf16[128,4096]{0,1:T(8,128)(2,1)S(1)}, bf16[128,4096]{0,1:T(8,128)(2,1)S(1)}, u32[]{:S(2)}, u32[]{:S(2)}) %collective-permute-start) | collective-permute-done | bytes 1048608 | tf_op jit(solution)/shard_map/while/body/eval_jaxpr/ppermute | solution.py:13
  501.4 9.4 %conditional.5 = ((bf16[128,4096]{0,1:T(8,128)(2,1)S(1)}, f32[8,128,1024]{1,2,0:T(8,128)})) conditional(s32[]{:T(128)} %convert_element_type.77, (bf16[128,4096]{0,1:T(8,128)(2,1)S(1)}, f32[8,128,1024]{1,2,0:T(8,128)}) %tuple.99, (pred[]{:T(512)}, s32[]{:T(128)}, bf16[8,128,4096]{1,2,0:T(8,128)(2,1)}, bf16[128,4096]{0,1:T(8,128)(2,1)S(1)}, ...), branch_computations={%region_10.10_spmd, %region_11.13_spmd} | conditional | flops 683499520 | bytes 35195972 | solution.py:159
  508.2 1.9 fusion.18
  512.7 15.2 %collective-permute-done = bf16[128,4096]{0,1:T(8,128)(2,1)S(1)} collective-permute-done((bf16[128,4096]{0,1:T(8,128)(2,1)S(1)}, bf16[128,4096]{0,1:T(8,128)(2,1)S(1)}, u32[]{:S(2)}, u32[]{:S(2)}) %collective-permute-start) | collective-permute-done | bytes 1048608 | tf_op jit(solution)/shard_map/while/body/eval_jaxpr/ppermute | solution.py:13
  528.0 9.4 %conditional.5 = ((bf16[128,4096]{0,1:T(8,128)(2,1)S(1)}, f32[8,128,1024]{1,2,0:T(8,128)})) conditional(s32[]{:T(128)} %convert_element_type.77, (bf16[128,4096]{0,1:T(8,128)(2,1)S(1)}, f32[8,128,1024]{1,2,0:T(8,128)}) %tuple.99, (pred[]{:T(512)}, s32[]{:T(128)}, bf16[8,128,4096]{1,2,0:T(8,128)(2,1)}, bf16[128,4096]{0,1:T(8,128)(2,1)S(1)}, ...), branch_computations={%region_10.10_spmd, %region_11.13_spmd} | conditional | flops 683499520 | bytes 35195972 | solution.py:159
  539.3 15.6 %collective-permute-done = bf16[128,4096]{0,1:T(8,128)(2,1)S(1)} collective-permute-done((bf16[128,4096]{0,1:T(8,128)(2,1)S(1)}, bf16[128,4096]{0,1:T(8,128)(2,1)S(1)}, u32[]{:S(2)}, u32[]{:S(2)}) %collective-permute-start) | collective-permute-done | bytes 1048608 | tf_op jit(solution)/shard_map/while/body/eval_jaxpr/ppermute | solution.py:13
  554.9 9.4 %conditional.5 = ((bf16[128,4096]{0,1:T(8,128)(2,1)S(1)}, f32[8,128,1024]{1,2,0:T(8,128)})) conditional(s32[]{:T(128)} %convert_element_type.77, (bf16[128,4096]{0,1:T(8,128)(2,1)S(1)}, f32[8,128,1024]{1,2,0:T(8,128)}) %tuple.99, (pred[]{:T(512)}, s32[]{:T(128)}, bf16[8,128,4096]{1,2,0:T(8,128)(2,1)}, bf16[128,4096]{0,1:T(8,128)(2,1)S(1)}, ...), branch_computations={%region_10.10_spmd, %region_11.13_spmd} | conditional | flops 683499520 | bytes 35195972 | solution.py:159
  561.7 1.9 fusion.18
  566.3 15.2 %collective-permute-done = bf16[128,4096]{0,1:T(8,128)(2,1)S(1)} collective-permute-done((bf16[128,4096]{0,1:T(8,128)(2,1)S(1)}, bf16[128,4096]{0,1:T(8,128)(2,1)S(1)}, u32[]{:S(2)}, u32[]{:S(2)}) %collective-permute-start) | collective-permute-done | bytes 1048608 | tf_op jit(solution)/shard_map/while/body/eval_jaxpr/ppermute | solution.py:13
  581.5 9.4 %conditional.5 = ((bf16[128,4096]{0,1:T(8,128)(2,1)S(1)}, f32[8,128,1024]{1,2,0:T(8,128)})) conditional(s32[]{:T(128)} %convert_element_type.77, (bf16[128,4096]{0,1:T(8,128)(2,1)S(1)}, f32[8,128,1024]{1,2,0:T(8,128)}) %tuple.99, (pred[]{:T(512)}, s32[]{:T(128)}, bf16[8,128,4096]{1,2,0:T(8,128)(2,1)}, bf16[128,4096]{0,1:T(8,128)(2,1)S(1)}, ...), branch_computations={%region_10.10_spmd, %region_11.13_spmd} | conditional | flops 683499520 | bytes 35195972 | solution.py:159
  592.8 15.5 %collective-permute-done = bf16[128,4096]{0,1:T(8,128)(2,1)S(1)} collective-permute-done((bf16[128,4096]{0,1:T(8,128)(2,1)S(1)}, bf16[128,4096]{0,1:T(8,128)(2,1)S(1)}, u32[]{:S(2)}, u32[]{:S(2)}) %collective-permute-start) | collective-permute-done | bytes 1048608 | tf_op jit(solution)/shard_map/while/body/eval_jaxpr/ppermute | solution.py:13
  608.4 9.4 %conditional.5 = ((bf16[128,4096]{0,1:T(8,128)(2,1)S(1)}, f32[8,128,1024]{1,2,0:T(8,128)})) conditional(s32[]{:T(128)} %convert_element_type.77, (bf16[128,4096]{0,1:T(8,128)(2,1)S(1)}, f32[8,128,1024]{1,2,0:T(8,128)}) %tuple.99, (pred[]{:T(512)}, s32[]{:T(128)}, bf16[8,128,4096]{1,2,0:T(8,128)(2,1)}, bf16[128,4096]{0,1:T(8,128)(2,1)S(1)}, ...), branch_computations={%region_10.10_spmd, %region_11.13_spmd} | conditional | flops 683499520 | bytes 35195972 | solution.py:159
  619.7 14.2 %collective-permute-done = bf16[128,4096]{0,1:T(8,128)(2,1)S(1)} collective-permute-done((bf16[128,4096]{0,1:T(8,128)(2,1)S(1)}, bf16[128,4096]{0,1:T(8,128)(2,1)S(1)}, u32[]{:S(2)}, u32[]{:S(2)}) %collective-permute-start) | collective-permute-done | bytes 1048608 | tf_op jit(solution)/shard_map/while/body/eval_jaxpr/ppermute | solution.py:13
  633.9 2.6 convert_element_type.56
  636.5 2.6 copy.72
  (171 shorter events, 117.4 us)
Async XLA Ops:
  0.0 30.9 %copy-start = (s32[16,8,128]{2,1,0:T(8,128)S(1)}, s32[16,8,128]{2,1,0:T(8,128)}, u32[]{:S(2)}) copy-start(s32[16,8,128]{2,1,0:T(8,128)} %param.16) | copy-start | bytes 196612
  11.0 70.0 %all-to-all-start = ((bf16[16,1,128,1024]{3,2,1,0:T(8,128)(2,1)}), bf16[16,1,128,1024]{3,2,1,0:T(8,128)(2,1)}, u32[]{:S(2)}, u32[]{:S(2)}) async-start(bf16[16,1,128,1024]{3,2,1,0:T(8,128)(2,1)} %bitcast_select_fusion.3), calls=%async_computation | async-start | bytes 8388608 | tf_op jit(solution)/shard_map/all_to_all | solution.py:116
  18.7 12.0 %copy-start.2 = (s32[16,8]{0,1:T(8,128)S(1)}, s32[16,8]{0,1:T(8,128)}, u32[]{:S(2)}) copy-start(s32[16,8]{0,1:T(8,128)} %param.17) | copy-start | bytes 1540
  96.1 17.7 %collective-permute-start = (bf16[128,4096]{0,1:T(8,128)(2,1)S(1)}, bf16[128,4096]{0,1:T(8,128)(2,1)S(1)}, u32[]{:S(2)}, u32[]{:S(2)}) collective-permute-start(bf16[128,4096]{0,1:T(8,128)(2,1)S(1)} %get-tuple-element.646), channel_id=1, source_target_pairs={{16,0},{32,16},{48,32},{64,48},{80,64},{96,80},{112,96},{128,112},... | collective-permute-start | bytes 3145736 | tf_op jit(solution)/shard_map/while/body/eval_jaxpr/ppermute | solution.py:13
  113.9 16.1 %collective-permute-start = (bf16[128,4096]{0,1:T(8,128)(2,1)S(1)}, bf16[128,4096]{0,1:T(8,128)(2,1)S(1)}, u32[]{:S(2)}, u32[]{:S(2)}) collective-permute-start(bf16[128,4096]{0,1:T(8,128)(2,1)S(1)} %get-tuple-element.646), channel_id=1, source_target_pairs={{16,0},{32,16},{48,32},{64,48},{80,64},{96,80},{112,96},{128,112},... | collective-permute-start | bytes 3145736 | tf_op jit(solution)/shard_map/while/body/eval_jaxpr/ppermute | solution.py:13
  130.0 16.1 %collective-permute-start = (bf16[128,4096]{0,1:T(8,128)(2,1)S(1)}, bf16[128,4096]{0,1:T(8,128)(2,1)S(1)}, u32[]{:S(2)}, u32[]{:S(2)}) collective-permute-start(bf16[128,4096]{0,1:T(8,128)(2,1)S(1)} %get-tuple-element.646), channel_id=1, source_target_pairs={{16,0},{32,16},{48,32},{64,48},{80,64},{96,80},{112,96},{128,112},... | collective-permute-start | bytes 3145736 | tf_op jit(solution)/shard_map/while/body/eval_jaxpr/ppermute | solution.py:13
  146.1 16.1 %collective-permute-start = (bf16[128,4096]{0,1:T(8,128)(2,1)S(1)}, bf16[128,4096]{0,1:T(8,128)(2,1)S(1)}, u32[]{:S(2)}, u32[]{:S(2)}) collective-permute-start(bf16[128,4096]{0,1:T(8,128)(2,1)S(1)} %get-tuple-element.646), channel_id=1, source_target_pairs={{16,0},{32,16},{48,32},{64,48},{80,64},{96,80},{112,96},{128,112},... | collective-permute-start | bytes 3145736 | tf_op jit(solution)/shard_map/while/body/eval_jaxpr/ppermute | solution.py:13
  162.2 16.1 %collective-permute-start = (bf16[128,4096]{0,1:T(8,128)(2,1)S(1)}, bf16[128,4096]{0,1:T(8,128)(2,1)S(1)}, u32[]{:S(2)}, u32[]{:S(2)}) collective-permute-start(bf16[128,4096]{0,1:T(8,128)(2,1)S(1)} %get-tuple-element.646), channel_id=1, source_target_pairs={{16,0},{32,16},{48,32},{64,48},{80,64},{96,80},{112,96},{128,112},... | collective-permute-start | bytes 3145736 | tf_op jit(solution)/shard_map/while/body/eval_jaxpr/ppermute | solution.py:13
  178.3 16.1 %collective-permute-start = (bf16[128,4096]{0,1:T(8,128)(2,1)S(1)}, bf16[128,4096]{0,1:T(8,128)(2,1)S(1)}, u32[]{:S(2)}, u32[]{:S(2)}) collective-permute-start(bf16[128,4096]{0,1:T(8,128)(2,1)S(1)} %get-tuple-element.646), channel_id=1, source_target_pairs={{16,0},{32,16},{48,32},{64,48},{80,64},{96,80},{112,96},{128,112},... | collective-permute-start | bytes 3145736 | tf_op jit(solution)/shard_map/while/body/eval_jaxpr/ppermute | solution.py:13
  194.4 16.1 %collective-permute-start = (bf16[128,4096]{0,1:T(8,128)(2,1)S(1)}, bf16[128,4096]{0,1:T(8,128)(2,1)S(1)}, u32[]{:S(2)}, u32[]{:S(2)}) collective-permute-start(bf16[128,4096]{0,1:T(8,128)(2,1)S(1)} %get-tuple-element.646), channel_id=1, source_target_pairs={{16,0},{32,16},{48,32},{64,48},{80,64},{96,80},{112,96},{128,112},... | collective-permute-start | bytes 3145736 | tf_op jit(solution)/shard_map/while/body/eval_jaxpr/ppermute | solution.py:13
  210.5 16.1 %collective-permute-start = (bf16[128,4096]{0,1:T(8,128)(2,1)S(1)}, bf16[128,4096]{0,1:T(8,128)(2,1)S(1)}, u32[]{:S(2)}, u32[]{:S(2)}) collective-permute-start(bf16[128,4096]{0,1:T(8,128)(2,1)S(1)} %get-tuple-element.646), channel_id=1, source_target_pairs={{16,0},{32,16},{48,32},{64,48},{80,64},{96,80},{112,96},{128,112},... | collective-permute-start | bytes 3145736 | tf_op jit(solution)/shard_map/while/body/eval_jaxpr/ppermute | solution.py:13
  226.6 16.1 %collective-permute-start = (bf16[128,4096]{0,1:T(8,128)(2,1)S(1)}, bf16[128,4096]{0,1:T(8,128)(2,1)S(1)}, u32[]{:S(2)}, u32[]{:S(2)}) collective-permute-start(bf16[128,4096]{0,1:T(8,128)(2,1)S(1)} %get-tuple-element.646), channel_id=1, source_target_pairs={{16,0},{32,16},{48,32},{64,48},{80,64},{96,80},{112,96},{128,112},... | collective-permute-start | bytes 3145736 | tf_op jit(solution)/shard_map/while/body/eval_jaxpr/ppermute | solution.py:13
  242.7 16.1 %collective-permute-start = (bf16[128,4096]{0,1:T(8,128)(2,1)S(1)}, bf16[128,4096]{0,1:T(8,128)(2,1)S(1)}, u32[]{:S(2)}, u32[]{:S(2)}) collective-permute-start(bf16[128,4096]{0,1:T(8,128)(2,1)S(1)} %get-tuple-element.646), channel_id=1, source_target_pairs={{16,0},{32,16},{48,32},{64,48},{80,64},{96,80},{112,96},{128,112},... | collective-permute-start | bytes 3145736 | tf_op jit(solution)/shard_map/while/body/eval_jaxpr/ppermute | solution.py:13
  258.8 16.1 %collective-permute-start = (bf16[128,4096]{0,1:T(8,128)(2,1)S(1)}, bf16[128,4096]{0,1:T(8,128)(2,1)S(1)}, u32[]{:S(2)}, u32[]{:S(2)}) collective-permute-start(bf16[128,4096]{0,1:T(8,128)(2,1)S(1)} %get-tuple-element.646), channel_id=1, source_target_pairs={{16,0},{32,16},{48,32},{64,48},{80,64},{96,80},{112,96},{128,112},... | collective-permute-start | bytes 3145736 | tf_op jit(solution)/shard_map/while/body/eval_jaxpr/ppermute | solution.py:13
  274.9 16.1 %collective-permute-start = (bf16[128,4096]{0,1:T(8,128)(2,1)S(1)}, bf16[128,4096]{0,1:T(8,128)(2,1)S(1)}, u32[]{:S(2)}, u32[]{:S(2)}) collective-permute-start(bf16[128,4096]{0,1:T(8,128)(2,1)S(1)} %get-tuple-element.646), channel_id=1, source_target_pairs={{16,0},{32,16},{48,32},{64,48},{80,64},{96,80},{112,96},{128,112},... | collective-permute-start | bytes 3145736 | tf_op jit(solution)/shard_map/while/body/eval_jaxpr/ppermute | solution.py:13
  291.0 16.1 %collective-permute-start = (bf16[128,4096]{0,1:T(8,128)(2,1)S(1)}, bf16[128,4096]{0,1:T(8,128)(2,1)S(1)}, u32[]{:S(2)}, u32[]{:S(2)}) collective-permute-start(bf16[128,4096]{0,1:T(8,128)(2,1)S(1)} %get-tuple-element.646), channel_id=1, source_target_pairs={{16,0},{32,16},{48,32},{64,48},{80,64},{96,80},{112,96},{128,112},... | collective-permute-start | bytes 3145736 | tf_op jit(solution)/shard_map/while/body/eval_jaxpr/ppermute | solution.py:13
  307.1 16.1 %collective-permute-start = (bf16[128,4096]{0,1:T(8,128)(2,1)S(1)}, bf16[128,4096]{0,1:T(8,128)(2,1)S(1)}, u32[]{:S(2)}, u32[]{:S(2)}) collective-permute-start(bf16[128,4096]{0,1:T(8,128)(2,1)S(1)} %get-tuple-element.646), channel_id=1, source_target_pairs={{16,0},{32,16},{48,32},{64,48},{80,64},{96,80},{112,96},{128,112},... | collective-permute-start | bytes 3145736 | tf_op jit(solution)/shard_map/while/body/eval_jaxpr/ppermute | solution.py:13
  323.2 97.7 %collective-permute-start = (bf16[128,4096]{0,1:T(8,128)(2,1)S(1)}, bf16[128,4096]{0,1:T(8,128)(2,1)S(1)}, u32[]{:S(2)}, u32[]{:S(2)}) collective-permute-start(bf16[128,4096]{0,1:T(8,128)(2,1)S(1)} %get-tuple-element.646), channel_id=1, source_target_pairs={{16,0},{32,16},{48,32},{64,48},{80,64},{96,80},{112,96},{128,112},... | collective-permute-start | bytes 3145736 | tf_op jit(solution)/shard_map/while/body/eval_jaxpr/ppermute | solution.py:13
  430.4 17.4 %collective-permute-start = (bf16[128,4096]{0,1:T(8,128)(2,1)S(1)}, bf16[128,4096]{0,1:T(8,128)(2,1)S(1)}, u32[]{:S(2)}, u32[]{:S(2)}) collective-permute-start(bf16[128,4096]{0,1:T(8,128)(2,1)S(1)} %get-tuple-element.646), channel_id=1, source_target_pairs={{16,0},{32,16},{48,32},{64,48},{80,64},{96,80},{112,96},{128,112},... | collective-permute-start | bytes 3145736 | tf_op jit(solution)/shard_map/while/body/eval_jaxpr/ppermute | solution.py:13
  457.2 17.5 %collective-permute-start = (bf16[128,4096]{0,1:T(8,128)(2,1)S(1)}, bf16[128,4096]{0,1:T(8,128)(2,1)S(1)}, u32[]{:S(2)}, u32[]{:S(2)}) collective-permute-start(bf16[128,4096]{0,1:T(8,128)(2,1)S(1)} %get-tuple-element.646), channel_id=1, source_target_pairs={{16,0},{32,16},{48,32},{64,48},{80,64},{96,80},{112,96},{128,112},... | collective-permute-start | bytes 3145736 | tf_op jit(solution)/shard_map/while/body/eval_jaxpr/ppermute | solution.py:13
  484.1 17.3 %collective-permute-start = (bf16[128,4096]{0,1:T(8,128)(2,1)S(1)}, bf16[128,4096]{0,1:T(8,128)(2,1)S(1)}, u32[]{:S(2)}, u32[]{:S(2)}) collective-permute-start(bf16[128,4096]{0,1:T(8,128)(2,1)S(1)} %get-tuple-element.646), channel_id=1, source_target_pairs={{16,0},{32,16},{48,32},{64,48},{80,64},{96,80},{112,96},{128,112},... | collective-permute-start | bytes 3145736 | tf_op jit(solution)/shard_map/while/body/eval_jaxpr/ppermute | solution.py:13
  510.8 17.2 %collective-permute-start = (bf16[128,4096]{0,1:T(8,128)(2,1)S(1)}, bf16[128,4096]{0,1:T(8,128)(2,1)S(1)}, u32[]{:S(2)}, u32[]{:S(2)}) collective-permute-start(bf16[128,4096]{0,1:T(8,128)(2,1)S(1)} %get-tuple-element.646), channel_id=1, source_target_pairs={{16,0},{32,16},{48,32},{64,48},{80,64},{96,80},{112,96},{128,112},... | collective-permute-start | bytes 3145736 | tf_op jit(solution)/shard_map/while/body/eval_jaxpr/ppermute | solution.py:13
  537.4 17.5 %collective-permute-start = (bf16[128,4096]{0,1:T(8,128)(2,1)S(1)}, bf16[128,4096]{0,1:T(8,128)(2,1)S(1)}, u32[]{:S(2)}, u32[]{:S(2)}) collective-permute-start(bf16[128,4096]{0,1:T(8,128)(2,1)S(1)} %get-tuple-element.646), channel_id=1, source_target_pairs={{16,0},{32,16},{48,32},{64,48},{80,64},{96,80},{112,96},{128,112},... | collective-permute-start | bytes 3145736 | tf_op jit(solution)/shard_map/while/body/eval_jaxpr/ppermute | solution.py:13
  564.3 17.1 %collective-permute-start = (bf16[128,4096]{0,1:T(8,128)(2,1)S(1)}, bf16[128,4096]{0,1:T(8,128)(2,1)S(1)}, u32[]{:S(2)}, u32[]{:S(2)}) collective-permute-start(bf16[128,4096]{0,1:T(8,128)(2,1)S(1)} %get-tuple-element.646), channel_id=1, source_target_pairs={{16,0},{32,16},{48,32},{64,48},{80,64},{96,80},{112,96},{128,112},... | collective-permute-start | bytes 3145736 | tf_op jit(solution)/shard_map/while/body/eval_jaxpr/ppermute | solution.py:13
  590.9 17.5 %collective-permute-start = (bf16[128,4096]{0,1:T(8,128)(2,1)S(1)}, bf16[128,4096]{0,1:T(8,128)(2,1)S(1)}, u32[]{:S(2)}, u32[]{:S(2)}) collective-permute-start(bf16[128,4096]{0,1:T(8,128)(2,1)S(1)} %get-tuple-element.646), channel_id=1, source_target_pairs={{16,0},{32,16},{48,32},{64,48},{80,64},{96,80},{112,96},{128,112},... | collective-permute-start | bytes 3145736 | tf_op jit(solution)/shard_map/while/body/eval_jaxpr/ppermute | solution.py:13
  617.8 16.1 %collective-permute-start = (bf16[128,4096]{0,1:T(8,128)(2,1)S(1)}, bf16[128,4096]{0,1:T(8,128)(2,1)S(1)}, u32[]{:S(2)}, u32[]{:S(2)}) collective-permute-start(bf16[128,4096]{0,1:T(8,128)(2,1)S(1)} %get-tuple-element.646), channel_id=1, source_target_pairs={{16,0},{32,16},{48,32},{64,48},{80,64},{96,80},{112,96},{128,112},... | collective-permute-start | bytes 3145736 | tf_op jit(solution)/shard_map/while/body/eval_jaxpr/ppermute | solution.py:13
  633.9 5.2 copy-start.1
where the time goes:
time: 642 us; the launch traced here: 639 us
  waiting for transfers between devices  465 us (72%)
  starting transfers between devices  53.4 us (8%)
  local copies, waits for them, and re-layouts  53.1 us (8%)
  other arithmetic  43.3 us (7%)
  matrix products  22.5 us (4%)
    ppermute x23, waiting for transfers between devices, from_behind(): return lax.ppermute(block, axis, route)  416 us
    all_to_all x1, waiting for transfers between devices, on_device(): lax.all_to_all(outgoing, 'dp', split_axis=0, concat_axis=0, tiled=True)  49.2 us
    ppermute x23, starting transfers between devices, from_behind(): return lax.ppermute(block, axis, route)  45.8 us
    unnamed x8, local copies, waits for them, and re-layouts  15.9 us
    dynamic_update_slice x8, other arithmetic, backward_unit(): lax.dynamic_update_index_in_dim(results_old, pick_row(results_old, micro_...  15.4 us
  transfers between devices with their start and end apart: 24, of which 24 were waited for; matrix products, arithmetic and copies ran while one was open for 2% of the time, Pallas kernels for 0%

commit v1 on v0

v1 whole, which is shorter than its diff:
```python
import functools

import jax
import jax.numpy as jnp
from jax import lax
from jax.experimental import pallas as pl
from jax.experimental.pallas import tpu as pltpu
from jax.sharding import PartitionSpec as P

MESH = pl.DeviceIdType.MESH
SIDE = 4
REPLICAS = SIDE * SIDE
HEAD = 128
GROUP = 8
MICRO = 8
SEQ = 128
CHUNK = 32
QUARTERS = SEQ // CHUNK
HEADS_HERE = 2
PHASES = HEADS_HERE * QUARTERS
UNITS = PHASES * MICRO
COLUMNS = GROUP * CHUNK
SCALE = HEAD**-0.5
LOG2E = 1.4426950408889634
CHIPS_DEEP = 8
OFFSETS = (
    (2, 2), (2, 1), (1, 2), (2, 3), (3, 2), (1, 1), (3, 3), (1, 3),
    (3, 1), (0, 2), (2, 0), (0, 1), (1, 0), (0, 3), (3, 0),
)


def dot(a, b, contract):
    return lax.dot_general(a, b, ((contract[:1], contract[1:]), ((), ())), preferred_element_type=jnp.float32)


def kernel(assign, q_hbm, kv_hbm, weights, docs, out, *scratch):
    (raw, outgoing, selected, queries, grads_in, grads_out, total, staged, doc_columns, doc_rows, weight_rows) = scratch[:11]
    arriving = scratch[11 : 11 + PHASES]
    (raw_sem, query_own, query_send, query_recv, slot_send, slot_send_twin, slot_recv, grad_send, grad_recv,
     out_own, out_send, out_recv) = scratch[11 + PHASES :]

    section, me = lax.axis_index("section"), lax.axis_index("dp")
    core = lax.rem(section, 2)
    deep = section // 2
    twin = section + 1 - 2 * core
    other = 1 - core
    y, x = me // SIDE, lax.rem(me, SIDE)
    is_top, is_bottom = deep == CHIPS_DEEP - 1, deep == 0

    def replica_at(dy, dx):
        return lax.rem(y + dy, SIDE) * SIDE + lax.rem(x + dx, SIDE)

    load_raw = pltpu.make_async_copy(kv_hbm, raw, raw_sem)
    load_raw.start()
    own_queries = []
    for a in range(HEADS_HERE):
        column = pl.multiple_of((core * HEADS_HERE + a) * GROUP * HEAD, HEAD)
        copy = pltpu.make_async_copy(
            q_hbm.at[:, :, pl.ds(column, GROUP * HEAD)], queries.at[core, a], query_own.at[a]
        )
        copy.start()
        own_queries.append(copy)

    barrier = pltpu.get_barrier_semaphore()
    for dy, dx in OFFSETS:
        for where in (section, twin):
            pl.semaphore_signal(barrier, inc=1, device_id=(where, replica_at(dy, dx)), device_id_type=MESH)
    pl.semaphore_signal(barrier, inc=1, device_id=(twin, me), device_id_type=MESH)

    @pl.when(jnp.logical_not(is_bottom))
    def _():
        pl.semaphore_signal(barrier, inc=1, device_id=(section - 2, me), device_id_type=MESH)

    @pl.when(jnp.logical_not(is_top))
    def _():
        pl.semaphore_signal(barrier, inc=1, device_id=(section + 2, me), device_id_type=MESH)

    given = [assign[me, m] for m in range(MICRO)]
    slot_rows = []
    for k in range(REPLICAS):
        target = replica_at(k // SIDE, k % SIDE)
        row = 0
        for m in range(MICRO):
            row = jnp.where(given[m] == target, m, row)
        slot_rows.append(row)
    sources, slots = [], []
    for m in range(MICRO):
        source = 0
        for s in range(REPLICAS):
            source = jnp.where(assign[s, m] == me, s, source)
        sources.append(source)
        slots.append(
            lax.rem(y - source // SIDE + SIDE, SIDE) * SIDE + lax.rem(x - lax.rem(source, SIDE) + SIDE, SIDE)
        )

    def pack(p):
        a, q = divmod(p, QUARTERS)
        for k in range(REPLICAS):
            for c in range(2):
                for t in range(2):
                    column = (t * 2 * HEADS_HERE + c * HEADS_HERE + a) * HEAD
                    outgoing[p, k, c, :, t * HEAD : (t + 1) * HEAD] = raw[
                        slot_rows[k], q * CHUNK : (q + 1) * CHUNK, column : column + HEAD
                    ]

    def slot_copy(p, k, c, where, target, send_sem):
        return pltpu.make_async_remote_copy(
            src_ref=outgoing.at[p, k, c],
            dst_ref=arriving[p].at[core, k],
            send_sem=send_sem.at[p],
            recv_sem=slot_recv.at[p],
            device_id=(where, target),
            device_id_type=MESH,
        )

    def send(p):
        for dy, dx in OFFSETS:
            for c, where in ((core, section), (other, twin)):
                slot_copy(p, dy * SIDE + dx, c, where, replica_at(dy, dx), slot_send).start()
        slot_copy(p, 0, other, twin, me, slot_send_twin).start()
        pltpu.make_async_copy(outgoing.at[p, 0, core], arriving[p].at[core, 0], slot_recv.at[p]).start()

    def query_copy(a):
        column = pl.multiple_of((other * HEADS_HERE + a) * GROUP * HEAD, HEAD)
        return pltpu.make_async_remote_copy(
            src_ref=q_hbm.at[:, :, pl.ds(column, GROUP * HEAD)],
            dst_ref=queries.at[core, a],
            send_sem=query_send.at[a],
            recv_sem=query_recv.at[a],
            device_id=(twin, me),
            device_id_type=MESH,
        )

    def query_wait(a):
        return pltpu.make_async_remote_copy(
            src_ref=q_hbm.at[:, :, pl.ds(0, GROUP * HEAD)],
            dst_ref=queries.at[other, a],
            send_sem=query_send.at[a],
            recv_sem=query_recv.at[a],
            device_id=(twin, me),
            device_id_type=MESH,
        )

    load_raw.wait()
    pack(0)
    others = 2 * len(OFFSETS) + 1
    pl.semaphore_wait(barrier, others + jnp.where(is_bottom, 0, 1) + jnp.where(is_top, 0, 1))
    send(0)
    query_copy(0).start()
    for p in range(1, 3):
        pack(p)
        send(p)
    query_copy(1).start()

    lane = lax.broadcasted_iota(jnp.int32, (MICRO, SEQ), 1)
    run_docs = jnp.concatenate([docs[sources[m], m : m + 1, :] for m in range(MICRO)], axis=0)
    run_weights = jnp.concatenate([weights[0:1, m * SEQ : (m + 1) * SEQ] for m in range(MICRO)], axis=0)
    for q in range(QUARTERS):
        here = lane // CHUNK == q
        for held, rows in ((run_docs, doc_rows), (run_weights, weight_rows)):
            part = jnp.where(here, held, jnp.zeros_like(held))
            part = part + pltpu.roll(part, CHUNK, 1)
            rows[q] = part + pltpu.roll(part, 2 * CHUNK, 1)
    for m in range(MICRO):
        doc_columns[m] = jnp.broadcast_to(run_docs[m : m + 1], (SEQ, SEQ)).T

    for a in range(HEADS_HERE):
        for q in range(QUARTERS):
            p = a * QUARTERS + q
            if p >= 1 and p + 2 < PHASES:
                pack(p + 2)
                send(p + 2)
            pltpu.make_async_copy(arriving[p], arriving[p], slot_recv.at[p]).wait()
            for m in range(MICRO):
                for b in range(2):
                    selected[b, a, m, q * CHUNK : (q + 1) * CHUNK, :] = arriving[p][b, slots[m]]
            if q == 0:
                own_queries[a].wait()
                query_wait(a).wait_recv()
            first = max(0, q - 2) * CHUNK
            span = (q + 1) * CHUNK - first

            def unit(m, carry, a=a, q=q, p=p, first=first, span=span):
                u = p * MICRO + m
                key_row = lax.broadcasted_iota(jnp.int32, (span, SEQ), 0) + first
                query_row = lax.rem(lax.broadcasted_iota(jnp.int32, (span, SEQ), 1), CHUNK) + q * CHUNK
                same = doc_columns[m, first : first + span, :] == doc_rows[q, pl.ds(m, 1), :]
                bias = jnp.where(same & (key_row <= query_row), 0.0, -1e30)
                bias = jnp.concatenate([bias] * (COLUMNS // SEQ), axis=1)

                units_queries, keys, values, probs = [], [], [], []
                for b in range(2):
                    own = jnp.concatenate(
                        [
                            queries[b, a, m, q * CHUNK : (q + 1) * CHUNK, h * HEAD : (h + 1) * HEAD]
                            for h in range(GROUP)
                        ],
                        axis=0,
                    )
                    key = selected[b, a, m, first : first + span, 0:HEAD]
                    value = selected[b, a, m, first : first + span, HEAD : 2 * HEAD]
                    scores = dot(key, own, (1, 1))
                    soft = jnp.exp2(scores * (SCALE * LOG2E) + bias)
                    prob = soft * (1.0 / jnp.sum(soft, axis=0, keepdims=True))
                    units_queries.append(own)
                    keys.append(key)
                    values.append(value)
                    probs.append(prob)

                @pl.when(is_top)
                def _():
                    b = 1
                    eye = jnp.where(
                        lax.broadcasted_iota(jnp.int32, (HEAD, HEAD), 0)
                        == lax.broadcasted_iota(jnp.int32, (HEAD, HEAD), 1),
                        1.0,
                        0.0,
                    ).astype(jnp.bfloat16)
                    mixed = dot(values[b], probs[b].astype(jnp.bfloat16), (0, 0))
                    flat = dot(eye, units_queries[b], (1, 1))
                    weight = weight_rows[q, pl.ds(m, 1), :]
                    weight = jnp.concatenate([weight] * (COLUMNS // SEQ), axis=1)
                    grads_in[u] = (weight * (flat + mixed)).astype(jnp.bfloat16)

                @pl.when(jnp.logical_not(is_top))
                def _():
                    pltpu.make_async_remote_copy(
                        src_ref=grads_out.at[u],
                        dst_ref=grads_in.at[u],
                        send_sem=grad_send,
                        recv_sem=grad_recv.at[u],
                        device_id=(section, me),
                        device_id_type=MESH,
                    ).wait_recv()

                grads, score_grads = [None, grads_in[u]], [None, None]
                for b in (1, 0):
                    upstream = grads[b]
                    prob_grads = dot(values[b], upstream, (1, 0))
                    delta = jnp.sum(probs[b] * prob_grads, axis=0, keepdims=True)
                    score_grads[b] = (probs[b] * (prob_grads - delta)).astype(jnp.bfloat16)
                    if b == 1:
                        moved = dot(keys[b], score_grads[b], (0, 0)) * SCALE
                        grads[0] = (upstream.astype(jnp.float32) + moved).astype(jnp.bfloat16)

                @pl.when(jnp.logical_not(is_bottom))
                def _():
                    moved = dot(keys[0], score_grads[0], (0, 0)) * SCALE
                    grads_out[u] = (grads[0].astype(jnp.float32) + moved).astype(jnp.bfloat16)
                    pltpu.make_async_remote_copy(
                        src_ref=grads_out.at[u],
                        dst_ref=grads_in.at[u],
                        send_sem=grad_send,
                        recv_sem=grad_recv.at[u],
                        device_id=(section - 2, me),
                        device_id_type=MESH,
                    ).start()

                old = span - CHUNK
                for b in (1, 0):
                    key_term = dot(score_grads[b], units_queries[b], (1, 0)) * SCALE
                    value_term = dot(probs[b].astype(jnp.bfloat16), grads[b], (1, 1))
                    for t, term in ((0, key_term), (1, value_term)):
                        lanes = slice(t * HEAD, (t + 1) * HEAD)
                        if old:
                            total[b, m, first : first + old, lanes] += term[:old]
                        total[b, m, q * CHUNK : (q + 1) * CHUNK, lanes] = term[old:]
                        if q == QUARTERS - 1:
                            staged[b, a, m, t] = total[b, m, :, lanes].astype(jnp.bfloat16)
                if q == QUARTERS - 1:
                    for t in range(2):
                        column = pl.multiple_of((t * 2 * HEADS_HERE + core * HEADS_HERE + a) * HEAD, HEAD)
                        pltpu.make_async_copy(
                            staged.at[core, a, m, t], out.at[m, :, pl.ds(column, HEAD)], out_own
                        ).start()
                        pltpu.make_async_remote_copy(
                            src_ref=staged.at[other, a, m, t],
                            dst_ref=out.at[m, :, pl.ds(column, HEAD)],
                            send_sem=out_send,
                            recv_sem=out_recv,
                            device_id=(twin, me),
                            device_id_type=MESH,
                        ).start()
                return carry

            lax.fori_loop(0, MICRO, unit, 0)

    for p in range(PHASES):
        pltpu.make_async_copy(outgoing.at[p, pl.ds(1, REPLICAS - 1)], outgoing.at[p, pl.ds(1, REPLICAS - 1)], slot_send.at[p]).wait()
        pltpu.make_async_copy(outgoing.at[p, 0, 0], outgoing.at[p, 0, 0], slot_send_twin.at[p]).wait()
    for a in range(HEADS_HERE):
        query_copy(a).wait_send()

    @pl.when(jnp.logical_not(is_bottom))
    def _():
        pltpu.make_async_copy(grads_out, grads_out, grad_send).wait()

    pltpu.make_async_copy(staged.at[0], staged.at[0], out_own).wait()
    pltpu.make_async_copy(staged.at[0], staged.at[0], out_send).wait()
    pltpu.make_async_copy(staged.at[0], staged.at[0], out_recv).wait()


def on_device(layer_inputs, keys_values, loss_weight, doc_ids, assignment):
    features, width = layer_inputs.shape[-1], keys_values.shape[-1]
    bf16, f32, i32 = jnp.bfloat16, jnp.float32, jnp.int32
    dma = pltpu.SemaphoreType.DMA
    whole = pl.BlockSpec(memory_space=pltpu.VMEM)
    remote = pl.BlockSpec(memory_space=pl.ANY)
    grads = pl.pallas_call(
        kernel,
        out_shape=jax.ShapeDtypeStruct((MICRO, SEQ, width), bf16),
        in_specs=[pl.BlockSpec(memory_space=pltpu.SMEM), remote, remote, whole, whole],
        out_specs=remote,
        scratch_shapes=[
            pltpu.VMEM((MICRO, SEQ, width), bf16),
            pltpu.VMEM((PHASES, REPLICAS, 2, CHUNK, 2 * HEAD), bf16),
            pltpu.VMEM((2, HEADS_HERE, MICRO, SEQ, 2 * HEAD), bf16),
            pltpu.VMEM((2, HEADS_HERE, MICRO, SEQ, GROUP * HEAD), bf16),
            pltpu.VMEM((UNITS, HEAD, COLUMNS), bf16),
            pltpu.VMEM((UNITS, HEAD, COLUMNS), bf16),
            pltpu.VMEM((2, MICRO, SEQ, 2 * HEAD), f32),
            pltpu.VMEM((2, HEADS_HERE, MICRO, 2, SEQ, HEAD), bf16),
            pltpu.VMEM((MICRO, SEQ, SEQ), i32),
            pltpu.VMEM((QUARTERS, MICRO, SEQ), i32),
            pltpu.VMEM((QUARTERS, MICRO, SEQ), f32),
            *[pltpu.VMEM((2, REPLICAS, CHUNK, 2 * HEAD), bf16) for _ in range(PHASES)],
            dma,
            dma((HEADS_HERE,)),
            dma((HEADS_HERE,)),
            dma((HEADS_HERE,)),
            dma((PHASES,)),
            dma((PHASES,)),
            dma((PHASES,)),
            dma,
            dma((UNITS,)),
            dma,
            dma,
            dma,
        ],
        compiler_params=pltpu.CompilerParams(
            collective_id=0, has_side_effects=True, vmem_limit_bytes=50 << 20
        ),
    )(
        assignment,
        layer_inputs.reshape(MICRO, SEQ, features),
        keys_values.reshape(MICRO, SEQ, width),
        loss_weight,
        doc_ids,
    )
    return grads.reshape(1, 1, MICRO * SEQ, width)


def solution(mesh):
    placed = (
        P("section", "dp", None, None),
        P("section", "dp", None, None),
        P("dp", None),
        P(),
        P(),
    )
    return jax.shard_map(
        on_device,
        mesh=mesh,
        in_specs=placed,
        out_specs=P("section", "dp", None, None),
        check_vma=False,
    )
```

time: 642 us -> 145 us (0.23)
  waiting for transfers between devices: 465 us -> 0 us
  Pallas kernels: 0 us -> 141 us
  starting transfers between devices: 53.4 us -> 0 us
  local copies, waits for them, and re-layouts: 53.1 us -> 3.6 us
  other arithmetic: 43.3 us -> 0 us
  matrix products: 22.5 us -> 0 us
    ppermute x23 -> x0, waiting for transfers between devices: 416 us -> none  [from_behind(): return lax.ppermute(block, axis, route)]
    pallas_call x0 -> x1, Pallas kernels: none -> 141 us  [on_device(): pl.pallas_call(kernel, out_shape=jax.ShapeDtypeStruct((MICRO, SEQ, width)...]
    all_to_all x1 -> x0, waiting for transfers between devices: 49.2 us -> none  [on_device(): lax.all_to_all(outgoing, 'dp', split_axis=0, concat_axis=0, tiled=True)]
    ppermute x23 -> x0, starting transfers between devices: 45.8 us -> none  [from_behind(): return lax.ppermute(block, axis, route)]
    dot_general x40 -> x0, matrix products: 22.5 us -> none  [the longest x8 5.63 us: tile_backward(): jnp.einsum('ikgd,jkd->kgij', grad_heads, value_heads, preferred_element_t...]
    select_n x12 -> x0, other arithmetic: 16.9 us -> none  [the longest x8 10.7 us: backward_unit(): upstream = jnp.where(is_top, seeded, received)]
    dynamic_update_slice x8 -> x0, other arithmetic: 15.4 us -> none  [backward_unit(): lax.dynamic_update_index_in_dim(results_old, pick_row(results_old, micro_...]
    unnamed x8 -> x6, local copies, waits for them, and re-layouts: 15.9 us -> 3.6 us
  transfers between devices with their start and end apart: 24 -> 0, of which waited for: 24 -> 0; matrix products, arithmetic and copies ran while one was open for 2% -> 0% of each run, Pallas kernels for 0% -> 0%
where the time goes in v1:
time: 145 us
  Pallas kernels  141 us (97%)
  local copies, waits for them, and re-layouts  3.6 us (2%)
    pallas_call x1, Pallas kernels, on_device(): pl.pallas_call(kernel, out_shape=jax.ShapeDtypeStruct((MICRO, SEQ, width)...  141 us
    unnamed x6, local copies, waits for them, and re-layouts  3.6 us

profile of v1, /device:TPU:1, one launch (start us, length us, event | category | flops | bytes accessed | tf_op | source)
XLA Modules:
  0.0 145.1 jit_solution(999148318631129857)
XLA Ops:
  0.0 0.8 copy.6.assign
  0.8 0.0 copy-start
  0.8 0.8 copy-done
  1.6 0.0 copy-start.1
  1.6 0.7 copy-done.1
  2.3 141.4 %shard_map.55 = bf16[8,128,1024]{2,1,0:T(8,128)(2,1)S(1)} custom-call(s32[16,8]{1,0:T(8,128)S(1)} %copy.6.assign, bf16[8,128,4096]{2,1,0:T(8,128)(2,1)} %bitcast.4, bf16[8,128,1024]{2,1,0:T(8,128)(2,1)} %bitcast.5, f32[1,1024]{1,0:T(1,128)S(1)} %copy-done.1, s32[16,8,128]{2,1,0:T(8,128)S(1)} %copy-done), custom_call_target="tpu_custom_call" | custom-call | tf_op jit(solution)/shard_map/pallas_call | solution.py:309
  143.7 1.3 copy.8
Async XLA Ops:
  0.8 0.8 copy-start
  1.6 0.7 copy-start.1

commit v2 on v1

v2 whole, which is shorter than its diff:
```python
import functools

import jax
import jax.numpy as jnp
from jax import lax
from jax.experimental import pallas as pl
from jax.experimental.pallas import tpu as pltpu
from jax.sharding import PartitionSpec as P

MESH = pl.DeviceIdType.MESH
SIDE = 4
REPLICAS = SIDE * SIDE
HEAD = 128
GROUP = 8
MICRO = 8
SEQ = 128
HEADS_HERE = 2
BLOCK = 16
REACH = 64
PHASES = ((0, 0, 32), (0, 32, 32), (0, 64, 32), (0, 96, 32), (1, 0, 32), (1, 32, 32), (1, 64, 32), (1, 96, 32))
TOGETHER = 4
AHEAD = 3
BLOCKS = sum(rows // BLOCK for _, _, rows in PHASES) * MICRO
WIDEST = max(rows for _, _, rows in PHASES)
SCALE = HEAD**-0.5
LOG2E = 1.4426950408889634
CHIPS_DEEP = 8
OFFSETS = (
    (2, 2), (2, 1), (1, 2), (2, 3), (3, 2), (1, 1), (3, 3), (1, 3),
    (3, 1), (0, 2), (2, 0), (0, 1), (1, 0), (0, 3), (3, 0),
)


def dot(a, b, contract):
    return lax.dot_general(a, b, ((contract[:1], contract[1:]), ((), ())), preferred_element_type=jnp.float32)


def kernel(assign_hbm, q_hbm, kv_hbm, weights_hbm, docs_hbm, out, *scratch):
    (assign, slot_rows, weights, docs, raw, outgoing, selected, queries, grads_in, grads_out, total, staged, probs_held,
     doc_columns, doc_rows, weight_rows) = scratch[:16]
    arriving = scratch[16 : 16 + len(PHASES)]
    (small_sem, raw_sem, query_own, query_send, query_recv, slot_send, slot_recv, grad_send, grad_recv,
     out_own, out_send, out_recv) = scratch[16 + len(PHASES) :]

    section, me = lax.axis_index("section"), lax.axis_index("dp")
    core = lax.rem(section, 2)
    deep = section // 2
    twin = section + 1 - 2 * core
    other = 1 - core
    y, x = me // SIDE, lax.rem(me, SIDE)
    is_top, is_bottom = deep == CHIPS_DEEP - 1, deep == 0

    def replica_at(dy, dx):
        return lax.rem(y + dy, SIDE) * SIDE + lax.rem(x + dx, SIDE)

    loads = [
        pltpu.make_async_copy(source, held, small_sem.at[i])
        for i, (source, held) in enumerate(((assign_hbm, assign), (weights_hbm, weights), (docs_hbm, docs)))
    ]
    for load in loads:
        load.start()
    load_raw = pltpu.make_async_copy(kv_hbm, raw, raw_sem)
    load_raw.start()
    barrier = pltpu.get_barrier_semaphore()
    for dy, dx in OFFSETS:
        for where in (section, twin):
            pl.semaphore_signal(barrier, inc=1, device_id=(where, replica_at(dy, dx)), device_id_type=MESH)
    pl.semaphore_signal(barrier, inc=1, device_id=(twin, me), device_id_type=MESH)

    @pl.when(jnp.logical_not(is_bottom))
    def _():
        pl.semaphore_signal(barrier, inc=1, device_id=(section - 2, me), device_id_type=MESH)

    @pl.when(jnp.logical_not(is_top))
    def _():
        pl.semaphore_signal(barrier, inc=1, device_id=(section + 2, me), device_id_type=MESH)

    for load in loads:
        load.wait()
    given = [assign[m, me] for m in range(MICRO)]
    for k in range(REPLICAS):
        target = replica_at(k // SIDE, k % SIDE)
        row = 0
        for m in range(MICRO):
            row = jnp.where(given[m] == target, m, row)
        slot_rows[k] = row
    sources, slots = [], []
    for m in range(MICRO):
        source = 0
        for s in range(REPLICAS):
            source = jnp.where(assign[m, s] == me, s, source)
        sources.append(source)
        slots.append(
            lax.rem(y - source // SIDE + SIDE, SIDE) * SIDE + lax.rem(x - lax.rem(source, SIDE) + SIDE, SIDE)
        )

    def pack(p, k):
        a, start, rows = PHASES[p]
        row = slot_rows[k]
        for c in range(2):
            for t in range(2):
                column = (t * 2 * HEADS_HERE + c * HEADS_HERE + a) * HEAD
                outgoing[p, k, c, 0:rows, t * HEAD : (t + 1) * HEAD] = raw[row, start : start + rows, column : column + HEAD]

    def slot_copy(p, k, c, where, target, kind):
        return pltpu.make_async_remote_copy(
            src_ref=outgoing.at[p, k, c, pl.ds(0, PHASES[p][2])],
            dst_ref=arriving[p].at[core, k],
            send_sem=slot_send.at[p, kind],
            recv_sem=slot_recv.at[p],
            device_id=(where, target),
            device_id_type=MESH,
        )

    def keep(p):
        pltpu.make_async_copy(
            outgoing.at[p, 0, core, pl.ds(0, PHASES[p][2])], arriving[p].at[core, 0], slot_recv.at[p]
        ).start()

    def send(p):
        for dy, dx in OFFSETS:
            for c, where in ((core, section), (other, twin)):
                slot_copy(p, dy * SIDE + dx, c, where, replica_at(dy, dx), 0).start()
        slot_copy(p, 0, other, twin, me, 1).start()
        keep(p)

    def send_part(p, m):
        for k in (2 * m, 2 * m + 1):
            pack(p, k)
        for k in (2 * m, 2 * m + 1):
            target = replica_at(k // SIDE, lax.rem(k, SIDE))
            slot_copy(p, k, other, twin, target, jnp.where(k == 0, 1, 0)).start()

            @pl.when(k > 0)
            def _():
                slot_copy(p, k, core, section, target, 0).start()

        @pl.when(m == 0)
        def _():
            keep(p)

    def query_part(p, c):
        a, start, rows = PHASES[p]
        column = pl.multiple_of((c * HEADS_HERE + a) * GROUP * HEAD, HEAD)
        return q_hbm.at[:, pl.ds(start, rows), pl.ds(column, GROUP * HEAD)]

    def query_place(p, b):
        a, start, rows = PHASES[p]
        return queries.at[b, a, :, pl.ds(start, rows)]

    def query_copy(p, b):
        return pltpu.make_async_remote_copy(
            src_ref=query_part(p, other),
            dst_ref=query_place(p, b),
            send_sem=query_send.at[p],
            recv_sem=query_recv.at[p],
            device_id=(twin, me),
            device_id_type=MESH,
        )

    def query_load(p):
        return pltpu.make_async_copy(query_part(p, core), query_place(p, core), query_own.at[p])

    def query_start(p):
        query_load(p).start()
        query_copy(p, core).start()

    load_raw.wait()
    for k in range(REPLICAS):
        pack(0, k)
    others = 2 * len(OFFSETS) + 1
    pl.semaphore_wait(barrier, others + jnp.where(is_bottom, 0, 1) + jnp.where(is_top, 0, 1))
    send(0)
    query_start(0)
    for p in range(1, AHEAD):
        for k in range(REPLICAS):
            pack(p, k)
        send(p)
        query_start(p)

    lane = lax.broadcasted_iota(jnp.int32, (MICRO, SEQ), 1)
    run_docs = jnp.concatenate([docs[sources[m], m : m + 1, :] for m in range(MICRO)], axis=0)
    run_weights = jnp.concatenate([weights[0:1, m * SEQ : (m + 1) * SEQ] for m in range(MICRO)], axis=0)
    for i in range(SEQ // BLOCK):
        here = lane // BLOCK == i
        for held, table in ((run_docs, doc_rows), (run_weights, weight_rows)):
            part = jnp.where(here, held, jnp.zeros_like(held))
            part = pltpu.roll(part, SEQ - i * BLOCK, 1) if i else part
            step = BLOCK
            while step < SEQ:
                part = part + pltpu.roll(part, step, 1)
                step *= 2
            table[i] = part
    for m in range(MICRO):
        doc_columns[m] = jnp.broadcast_to(run_docs[m : m + 1], (SEQ, SEQ)).T

    base = 0
    for p, (a, start, rows) in enumerate(PHASES):
        pltpu.make_async_copy(arriving[p], arriving[p], slot_recv.at[p]).wait()
        for m in range(MICRO):
            for b in range(2):
                selected[b, a, m, start : start + rows, :] = arriving[p][b, slots[m]]
        query_load(p).wait()
        query_copy(p, other).wait_recv()
        if p >= 1 and p + 2 < len(PHASES):
            query_start(p + 2)
        blocks = range(start // BLOCK, (start + rows) // BLOCK)
        first = max(0, (start - REACH + 1) // BLOCK * BLOCK)
        span = start + rows - first
        old = span - rows
        parts = rows // BLOCK
        last = start + rows == SEQ
        done = SEQ if last else max(0, (PHASES[p + 1][1] - REACH + 1) // BLOCK * BLOCK)

        def beside(pieces):
            return jnp.concatenate(pieces, axis=1) if len(pieces) > 1 else pieces[0]

        def queries_of(b, m, a=a, blocks=blocks):
            return jnp.concatenate(
                [
                    queries[b, a, m, i * BLOCK : (i + 1) * BLOCK, h * HEAD : (h + 1) * HEAD]
                    for i in blocks
                    for h in range(GROUP)
                ],
                axis=0,
            )

        def keys_of(b, m, a=a, first=first, span=span):
            return selected[b, a, m, first : first + span, 0:HEAD]

        def values_of(b, m, a=a, first=first, span=span):
            return selected[b, a, m, first : first + span, HEAD : 2 * HEAD]

        def find_probs(m, blocks=blocks, first=first, span=span, rows=rows, beside=beside):
            key_row = lax.broadcasted_iota(jnp.int32, (span, SEQ), 0) + first
            query_row = lax.rem(lax.broadcasted_iota(jnp.int32, (span, SEQ), 1), BLOCK)
            key_docs = doc_columns[m, first : first + span, :]
            masks = [
                jnp.where(
                    (key_docs == doc_rows[i, pl.ds(m, 1), :]) & (key_row <= query_row + i * BLOCK), 0.0, -1e30
                )
                for i in blocks
            ]
            bias = beside(masks)
            for b in (1, 0):
                scores = dot(keys_of(b, m), queries_of(b, m), (1, 1))
                soft = jnp.exp2(scores * (SCALE * LOG2E) + bias)
                prob = soft * (1.0 / jnp.sum(soft, axis=0, keepdims=True))
                probs_held[lax.rem(m, 2), b, 0:span, 0 : GROUP * rows] = prob

        def unit(m, carry, p=p, a=a, start=start, rows=rows, span=span, first=first, old=old, parts=parts, last=last, done=done,
                 base=base, blocks=blocks, beside=beside):
            at = base + m * parts

            def grad_copy(where):
                return pltpu.make_async_remote_copy(
                    src_ref=grads_out.at[pl.ds(at, parts)],
                    dst_ref=grads_in.at[pl.ds(at, parts)],
                    send_sem=grad_send,
                    recv_sem=grad_recv.at[p, m],
                    device_id=(where, me),
                    device_id_type=MESH,
                )

            def put(ref, value):
                for i in range(parts):
                    ref[at + i] = value[:, i * SEQ : (i + 1) * SEQ]

            probs = [probs_held[lax.rem(m, 2), b, 0:span, 0 : GROUP * rows] for b in range(2)]

            @pl.when(is_top)
            def _():
                eye = jnp.where(
                    lax.broadcasted_iota(jnp.int32, (HEAD, HEAD), 0)
                    == lax.broadcasted_iota(jnp.int32, (HEAD, HEAD), 1),
                    1.0,
                    0.0,
                ).astype(jnp.bfloat16)
                mixed = dot(values_of(1, m), probs[1].astype(jnp.bfloat16), (0, 0))
                flat = dot(eye, queries_of(1, m), (1, 1))
                weight = beside([weight_rows[i, pl.ds(m, 1), :] for i in blocks])
                put(grads_in, (weight * (flat + mixed)).astype(jnp.bfloat16))

            @pl.when(jnp.logical_not(is_top))
            def _():
                grad_copy(section).wait_recv()

            upstream = beside([grads_in[at + i] for i in range(parts)])
            grads, score_grads = [None, upstream], [None, None]
            for b in (1, 0):
                prob = probs[b]
                prob_grads = dot(values_of(b, m), grads[b], (1, 0))
                delta = jnp.sum(prob * prob_grads, axis=0, keepdims=True)
                score_grads[b] = (prob * (prob_grads - delta)).astype(jnp.bfloat16)
                if b == 1:
                    moved = dot(keys_of(b, m), score_grads[b], (0, 0)) * SCALE
                    grads[0] = (upstream.astype(jnp.float32) + moved).astype(jnp.bfloat16)

            @pl.when(jnp.logical_not(is_bottom))
            def _():
                moved = dot(keys_of(0, m), score_grads[0], (0, 0)) * SCALE
                put(grads_out, (grads[0].astype(jnp.float32) + moved).astype(jnp.bfloat16))
                grad_copy(section - 2).start()

            for b in (1, 0):
                key_term = dot(score_grads[b], queries_of(b, m), (1, 0)) * SCALE
                value_term = dot(probs[b].astype(jnp.bfloat16), grads[b], (1, 1))
                for t, term in ((0, key_term), (1, value_term)):
                    lanes = slice(t * HEAD, (t + 1) * HEAD)
                    for low, high, seen in ((first, start, True), (start, start + rows, False)):
                        for begin, end, final in ((low, min(high, done), True), (max(low, done), high, False)):
                            if begin < end:
                                piece = term[begin - first : end - first]
                                if seen:
                                    piece = piece + total[b, m, begin:end, lanes]
                                if final:
                                    staged[b, a, t, m, begin:end] = piece.astype(jnp.bfloat16)
                                else:
                                    total[b, m, begin:end, lanes] = piece
            find_probs(jnp.minimum(m + 1, MICRO - 1))
            if last:

                @pl.when(lax.rem(m, TOGETHER) == TOGETHER - 1)
                def _():
                    some = pl.ds(m - (TOGETHER - 1), TOGETHER)
                    for t in range(2):
                        column = pl.multiple_of((t * 2 * HEADS_HERE + core * HEADS_HERE + a) * HEAD, HEAD)
                        place = out.at[some, :, pl.ds(column, HEAD)]
                        pltpu.make_async_copy(staged.at[core, a, t, some], place, out_own).start()
                        pltpu.make_async_remote_copy(
                            src_ref=staged.at[other, a, t, some],
                            dst_ref=place,
                            send_sem=out_send,
                            recv_sem=out_recv,
                            device_id=(twin, me),
                            device_id_type=MESH,
                        ).start()
            if p >= 1 and p + 2 < len(PHASES):
                send_part(p + 2, m)
            return carry

        find_probs(0)
        lax.fori_loop(0, MICRO, unit, 0)
        base += parts * MICRO

    for p, (_, _, rows) in enumerate(PHASES):
        for i, part in enumerate(
            (outgoing.at[p, pl.ds(1, REPLICAS - 1), :, pl.ds(0, rows)], outgoing.at[p, 0, 0, pl.ds(0, rows)])
        ):
            pltpu.make_async_copy(part, part, slot_send.at[p, i]).wait()
    for p in range(len(PHASES)):
        query_copy(p, core).wait_send()

    @pl.when(jnp.logical_not(is_bottom))
    def _():
        pltpu.make_async_copy(grads_out, grads_out, grad_send).wait()

    pltpu.make_async_copy(staged.at[0], staged.at[0], out_own).wait()
    pltpu.make_async_copy(staged.at[0], staged.at[0], out_send).wait()
    pltpu.make_async_copy(staged.at[0], staged.at[0], out_recv).wait()


def on_device(layer_inputs, keys_values, loss_weight, doc_ids, assignment):
    features, width = layer_inputs.shape[-1], keys_values.shape[-1]
    bf16, f32, i32 = jnp.bfloat16, jnp.float32, jnp.int32
    dma = pltpu.SemaphoreType.DMA
    remote = pl.BlockSpec(memory_space=pl.ANY)
    grads = pl.pallas_call(
        kernel,
        out_shape=jax.ShapeDtypeStruct((MICRO, SEQ, width), bf16),
        in_specs=[remote] * 5,
        out_specs=remote,
        scratch_shapes=[
            pltpu.SMEM((MICRO, REPLICAS), i32),
            pltpu.SMEM((REPLICAS,), i32),
            pltpu.VMEM((1, MICRO * SEQ), f32),
            pltpu.VMEM((REPLICAS, MICRO, SEQ), i32),
            pltpu.VMEM((MICRO, SEQ, width), bf16),
            pltpu.VMEM((len(PHASES), REPLICAS, 2, WIDEST, 2 * HEAD), bf16),
            pltpu.VMEM((2, HEADS_HERE, MICRO, SEQ, 2 * HEAD), bf16),
            pltpu.VMEM((2, HEADS_HERE, MICRO, SEQ, GROUP * HEAD), bf16),
            pltpu.VMEM((BLOCKS, HEAD, SEQ), bf16),
            pltpu.VMEM((BLOCKS, HEAD, SEQ), bf16),
            pltpu.VMEM((2, MICRO, SEQ, 2 * HEAD), f32),
            pltpu.VMEM((2, HEADS_HERE, 2, MICRO, SEQ, HEAD), bf16),
            pltpu.VMEM((2, 2, SEQ, GROUP * WIDEST), f32),
            pltpu.VMEM((MICRO, SEQ, SEQ), i32),
            pltpu.VMEM((SEQ // BLOCK, MICRO, SEQ), i32),
            pltpu.VMEM((SEQ // BLOCK, MICRO, SEQ), f32),
            *[pltpu.VMEM((2, REPLICAS, rows, 2 * HEAD), bf16) for _, _, rows in PHASES],
            dma((3,)),
            dma,
            dma((len(PHASES),)),
            dma((len(PHASES),)),
            dma((len(PHASES),)),
            dma((len(PHASES), 2)),
            dma((len(PHASES),)),
            dma,
            dma((len(PHASES), MICRO)),
            dma,
            dma,
            dma,
        ],
        compiler_params=pltpu.CompilerParams(
            collective_id=0, has_side_effects=True, vmem_limit_bytes=50 << 20
        ),
    )(
        pltpu.with_memory_space_constraint(assignment.T, pltpu.HBM),
        layer_inputs.reshape(MICRO, SEQ, features),
        keys_values.reshape(MICRO, SEQ, width),
        pltpu.with_memory_space_constraint(loss_weight, pltpu.HBM),
        pltpu.with_memory_space_constraint(doc_ids, pltpu.HBM),
    )
    return grads.reshape(1, 1, MICRO * SEQ, width)


def solution(mesh):
    placed = (
        P("section", "dp", None, None),
        P("section", "dp", None, None),
        P("dp", None),
        P(),
        P(),
    )
    return jax.shard_map(
        on_device,
        mesh=mesh,
        in_specs=placed,
        out_specs=P("section", "dp", None, None),
        check_vma=False,
    )
```

time: 145 us -> 143 us (0.986)
  local copies, waits for them, and re-layouts: 3.6 us -> 1.32 us
    unnamed x6 -> x1, local copies, waits for them, and re-layouts: 3.6 us -> 1.32 us
where the time goes in v2:
time: 143 us
  Pallas kernels  141 us (99%)
    pallas_call x1, Pallas kernels, on_device(): pl.pallas_call(kernel, out_shape=jax.ShapeDtypeStruct((MICRO, SEQ, width)...  141 us

profile of v2, /device:TPU:1, one launch (start us, length us, event | category | flops | bytes accessed | tf_op | source)
XLA Modules:
  0.0 142.7 jit_solution(14187087595656177296)
XLA Ops:
  0.0 141.4 %shard_map.55 = bf16[8,128,1024]{2,1,0:T(8,128)(2,1)S(1)} custom-call(s32[8,16]{1,0:T(8,128)} %bitcast.7, bf16[8,128,4096]{2,1,0:T(8,128)(2,1)} %bitcast.5, bf16[8,128,1024]{2,1,0:T(8,128)(2,1)} %bitcast.6, f32[1,1024]{1,0:T(1,128)} %weights_hbm.1, s32[16,8,128]{2,1,0:T(8,128)} %docs_hbm.1), custom_call_target="tpu_custom_call" | custom-call | tf_op jit(solution)/shard_map/pallas_call | solution.py:368
  141.4 1.3 copy.7

commit v3 on v2

--- a/solution.py
+++ b/solution.py
@@ -19,7 +19,7 @@
 REACH = 64
 PHASES = ((0, 0, 32), (0, 32, 32), (0, 64, 32), (0, 96, 32), (1, 0, 32), (1, 32, 32), (1, 64, 32), (1, 96, 32))
 TOGETHER = 4
-AHEAD = 3
+AHEAD = 2
 BLOCKS = sum(rows // BLOCK for _, _, rows in PHASES) * MICRO
 WIDEST = max(rows for _, _, rows in PHASES)
 SCALE = HEAD**-0.5
@@ -75,8 +75,7 @@
     def _():
         pl.semaphore_signal(barrier, inc=1, device_id=(section + 2, me), device_id_type=MESH)
 
-    for load in loads:
-        load.wait()
+    loads[0].wait()
     given = [assign[m, me] for m in range(MICRO)]
     for k in range(REPLICAS):
         target = replica_at(k // SIDE, k % SIDE)
@@ -84,15 +83,6 @@
         for m in range(MICRO):
             row = jnp.where(given[m] == target, m, row)
         slot_rows[k] = row
-    sources, slots = [], []
-    for m in range(MICRO):
-        source = 0
-        for s in range(REPLICAS):
-            source = jnp.where(assign[m, s] == me, s, source)
-        sources.append(source)
-        slots.append(
-            lax.rem(y - source // SIDE + SIDE, SIDE) * SIDE + lax.rem(x - lax.rem(source, SIDE) + SIDE, SIDE)
-        )
 
     def pack(p, k):
         a, start, rows = PHASES[p]
@@ -177,6 +167,18 @@
             pack(p, k)
         send(p)
         query_start(p)
+
+    for load in loads[1:]:
+        load.wait()
+    sources, slots = [], []
+    for m in range(MICRO):
+        source = 0
+        for s in range(REPLICAS):
+            source = jnp.where(assign[m, s] == me, s, source)
+        sources.append(source)
+        slots.append(
+            lax.rem(y - source // SIDE + SIDE, SIDE) * SIDE + lax.rem(x - lax.rem(source, SIDE) + SIDE, SIDE)
+        )
 
     lane = lax.broadcasted_iota(jnp.int32, (MICRO, SEQ), 1)
     run_docs = jnp.concatenate([docs[sources[m], m : m + 1, :] for m in range(MICRO)], axis=0)
@@ -202,7 +204,7 @@
                 selected[b, a, m, start : start + rows, :] = arriving[p][b, slots[m]]
         query_load(p).wait()
         query_copy(p, other).wait_recv()
-        if p >= 1 and p + 2 < len(PHASES):
+        if p + 2 < len(PHASES):
             query_start(p + 2)
         blocks = range(start // BLOCK, (start + rows) // BLOCK)
         first = max(0, (start - REACH + 1) // BLOCK * BLOCK)
@@ -335,7 +337,7 @@
                             device_id=(twin, me),
                             device_id_type=MESH,
                         ).start()
-            if p >= 1 and p + 2 < len(PHASES):
+            if p + 2 < len(PHASES):
                 send_part(p + 2, m)
             return carry
 

time: 143 us -> 143 us (level)
  no operation moved by 1% of the time
where the time goes in v3:
time: 143 us
  Pallas kernels  141 us (99%)
    pallas_call x1, Pallas kernels, on_device(): pl.pallas_call(kernel, out_shape=jax.ShapeDtypeStruct((MICRO, SEQ, width)...  141 us

profile of v3, /device:TPU:1, one launch (start us, length us, event | category | flops | bytes accessed | tf_op | source)
XLA Modules:
  0.0 142.7 jit_solution(3486603306521018082)
XLA Ops:
  0.0 141.4 %shard_map.55 = bf16[8,128,1024]{2,1,0:T(8,128)(2,1)S(1)} custom-call(s32[8,16]{1,0:T(8,128)} %bitcast.7, bf16[8,128,4096]{2,1,0:T(8,128)(2,1)} %bitcast.5, bf16[8,128,1024]{2,1,0:T(8,128)(2,1)} %bitcast.6, f32[1,1024]{1,0:T(1,128)} %weights_hbm.1, s32[16,8,128]{2,1,0:T(8,128)} %docs_hbm.1), custom_call_target="tpu_custom_call" | custom-call | tf_op jit(solution)/shard_map/pallas_call | solution.py:370
  141.4 1.3 copy.7
